TPU v7x, 32 devices: a whole 2x2x4 slice. The times are simulated.
32 devices in a mesh: tm: 4 (over z), lat: 8 (over y, x, core).
Axes of the slice: x: 2, y: 2, z: 4, core: 2. Of those that a mesh axis runs over, the one named last changes fastest.
Arguments:
- trajectory: float32 [4, 84, 32, 128], P('tm', None, 'lat'), may hold values from -6 to 6
- step_levels: int32 [5], replicated, may hold values from 0 to 63, as said below
- in_weight: bfloat16 [256, 84], replicated, may hold values from -0.625 to 0.625
- in_bias: float32 [256], replicated, may hold values from -4 to 4
- conv_weight: bfloat16 [2, 256, 2304], replicated, may hold values from -0.125 to 0.125
- cond_weight: bfloat16 [256, 1024], replicated, may hold values from -0.375 to 0.375
- out_weight: bfloat16 [84, 256], replicated, may hold values from -0.375 to 0.375
Outputs:
- advanced: float32 [4, 84, 32, 128], P('tm', None, 'lat')
Inputs may be any that keep to these rules, and one draw needn't show every extreme that they name: `step_levels`: strictly increasing; the first entry is 0 and the last is 63.
All inputs are finite; a program needn't handle non-finite values.
Results may differ from a plain program's by a relative error of at most 0.0055.
Values may be sent and summed in bfloat16 or wider, within the bound.
A program may use at most 64 MiB of HBM per device.

v0:
```python
import jax
import jax.numpy as jnp
from jax import lax
from jax.sharding import PartitionSpec as P

LEVELS = 64
ITERS = 2


sigma_top = 1.0
sigma_low = 0.02
rho_power = 7.0


def extended(block, sides, width):
    for axis, dim in sides:
        count = lax.axis_size(axis)
        forward = [(i, i + 1) for i in range(count - 1)]
        backward = [(target, source) for source, target in forward]
        low = lax.ppermute(
            lax.slice_in_dim(block, block.shape[dim] - width, None, axis=dim), axis, forward
        )
        high = lax.ppermute(lax.slice_in_dim(block, 0, width, axis=dim), axis, backward)
        block = jnp.concatenate([low, block, high], axis=dim)
    return block


def carried_in(value, axis, join, neutral):
    count, mine = (lax.axis_size(axis), lax.axis_index(axis))
    pieces = lax.all_gather(value, axis)
    subtotal = jnp.full_like(value, 0) + jnp.asarray(neutral, value.dtype)

    def hop(position, subtotal):
        longer = join(subtotal, pieces[position])
        return jnp.where(position < mine, longer, subtotal)

    return lax.fori_loop(0, count - 1, hop, subtotal)


def from_root(array, axis, root):
    mine = lax.axis_index(axis) == root
    return lax.psum(jnp.where(mine, array, jnp.zeros_like(array)), axis)


def level_sigma(levels):
    fraction = levels.astype(jnp.float32) / (LEVELS - 1)
    root_value = sigma_top ** (1.0 / rho_power) + fraction * (
        sigma_low ** (1.0 / rho_power) - sigma_top ** (1.0 / rho_power)
    )
    return root_value**rho_power


def conditions_of(sigma_now, cond_weight):
    freq_count = cond_weight.shape[0] // 2
    frequency = 100.0 ** (jnp.arange(freq_count).astype(jnp.float32) / freq_count)
    phases = jnp.log(sigma_now) / 4.0 * frequency
    embedding = jnp.concatenate([jnp.cos(phases), jnp.sin(phases)]).astype(jnp.bfloat16)[None, :]
    conditions = jnp.dot(embedding, cond_weight, preferred_element_type=jnp.float32)[0]
    return jnp.split(conditions, 4)


def convolve(padded, weight):
    row_count = padded.shape[1] - 2
    shifted = []
    for offset_row in range(3):
        for offset_col in (-1, 0, 1):
            shifted.append(
                jnp.roll(padded[:, offset_row : offset_row + row_count, :], -offset_col, axis=2)
            )
    columns_all = jnp.concatenate(shifted, axis=0)
    flattened = columns_all.reshape(columns_all.shape[0], -1)
    response = jnp.dot(weight, flattened, preferred_element_type=jnp.float32)
    return response.reshape(weight.shape[0], row_count, padded.shape[2])


def project(scaled, in_weight, in_bias):
    channels, row_count, columns = scaled.shape
    hidden = (
        jnp.dot(in_weight, scaled.reshape(channels, -1), preferred_element_type=jnp.float32)
        + in_bias[:, None]
    )
    return hidden.reshape(-1, row_count, columns)


def inside_rows(first_global, row_count, total_rows):
    global_rows = first_global + jnp.arange(row_count)
    inside = jnp.logical_and(global_rows >= 0, global_rows < total_rows)
    return inside[None, :, None]


def field_drift(
    current,
    sigma_now,
    sigma_next,
    in_weight,
    in_bias,
    conv_weight,
    cond_weight,
    out_weight,
    first_row,
    total_rows,
):
    scale_one, shift_one, scale_two, shift_two = conditions_of(sigma_now, cond_weight)
    variance = sigma_now * sigma_now + 0.25
    scaled = (current / jnp.sqrt(variance)).astype(jnp.bfloat16)
    channels, row_count, columns = current.shape
    widened = extended(scaled, (("lat", 1),), 2)
    hidden_zero = project(widened, in_weight, in_bias)
    hidden_zero = jnp.where(
        inside_rows(first_row - 2, row_count + 4, total_rows), hidden_zero, 0.0
    ).astype(jnp.bfloat16)
    response = convolve(hidden_zero, conv_weight[0])
    hidden_wide = jax.nn.silu(
        response * (1.0 + scale_one[:, None, None]) + shift_one[:, None, None]
    )
    padded_one = jnp.where(
        inside_rows(first_row - 1, row_count + 2, total_rows), hidden_wide, 0.0
    ).astype(jnp.bfloat16)
    hidden_one = padded_one[:, 1:-1, :]
    response = convolve(padded_one, conv_weight[1])
    hidden_two = hidden_one.astype(jnp.float32) + jax.nn.silu(
        response * (1.0 + scale_two[:, None, None]) + shift_two[:, None, None]
    )
    hidden_two = hidden_two.astype(jnp.bfloat16)
    network = jnp.dot(
        out_weight, hidden_two.reshape(hidden_two.shape[0], -1), preferred_element_type=jnp.float32
    )
    network = network.reshape(channels, row_count, columns)
    denoised = 0.25 / variance * current + 0.5 * sigma_now / jnp.sqrt(variance) * network
    return (current - denoised) * ((sigma_next - sigma_now) / sigma_now)


def add_pair(earlier_sum, later_sum):
    return earlier_sum + later_sum


def earlier_drifts(carried):
    return carried_in(carried, "tm", add_pair, jnp.zeros_like(carried))


def on_device(trajectory, step_levels, in_weight, in_bias, conv_weight, cond_weight, out_weight):
    time_slot = lax.axis_index("tm")
    lat_slot = lax.axis_index("lat")
    current = trajectory[0]
    row_count = current.shape[1]
    first_row = lat_slot * row_count
    total_rows = row_count * lax.axis_size("lat")
    bounds = lax.dynamic_slice_in_dim(step_levels, time_slot, 2)
    sigmas = level_sigma(bounds)
    sigma_now = sigmas[0]
    sigma_next = sigmas[1]
    anchor = from_root(current, "tm", 0)
    result = current
    for sweep in range(ITERS):
        drift_term = field_drift(
            current,
            sigma_now,
            sigma_next,
            in_weight,
            in_bias,
            conv_weight,
            cond_weight,
            out_weight,
            first_row,
            total_rows,
        )
        earlier = earlier_drifts(drift_term)
        if sweep + 1 < ITERS:
            current = earlier + anchor
        else:
            result = earlier + anchor + drift_term
    return result[None]


def solution(mesh):
    in_specs = (P("tm", None, "lat", None), P(), P(), P(), P(), P(), P())
    out_specs = P("tm", None, "lat", None)
    return jax.shard_map(
        on_device, mesh=mesh, in_specs=in_specs, out_specs=out_specs, check_vma=False
    )
```

profile of v0, /device:TPU:4, one launch (start us, length us, event | category | flops | bytes accessed | tf_op | source)
XLA Modules:
  0.0 93.3 jit_solution(11348579759873012992)
XLA Ops:
  6.6 0.8 add_power_fusion
  7.3 0.6 fusion.25
  9.2 1.6 %select_bitcast_fusion = (f32[84,4,128]{2,1,0:T(4,128)}, bf16[84,4,128]{2,1,0:T(4,128)(2,1)S(1)}) fusion(f32[1,84,4,128]{3,2,1,0:T(4,128)} %param.11, pred[]{:T(512)S(6)} %eq.3, f32[]{:T(128)S(6)} %sqrt.2), kind=kLoop, calls=%fused_computation.66 | loop fusion | flops 129024 | bytes 430085 | tf_op jit(solution)/shard_map/jit(_where)/select_n | solution.py:42
  10.8 0.1 fusion.24
  10.9 2.8 %collective-permute-start.1 = (bf16[84,2,128]{2,1,0:T(2,128)(2,1)S(1)}, bf16[84,2,128]{2,1,0:T(2,128)(2,1)S(1)}, u32[]{:S(2)}, u32[]{:S(2)}) collective-permute-start(bf16[84,2,128]{2,1,0:T(2,128)(2,1)S(1)} %get-tuple-element.266), channel_id=1, source_target_pairs={{1,0},{2,1},{3,2},{4,3},{5,4},{6,5},{7,6},{9,8},{10,9},{11,10},{12... | collective-permute-start | bytes 129032 | tf_op jit(solution)/shard_map/ppermute | solution.py:23
  13.7 1.9 %collective-permute-start = (bf16[84,2,128]{2,1,0:T(2,128)(2,1)S(1)}, bf16[84,2,128]{2,1,0:T(2,128)(2,1)S(1)}, u32[]{:S(2)}, u32[]{:S(2)}) collective-permute-start(bf16[84,2,128]{2,1,0:T(2,128)(2,1)S(1)} %get-tuple-element.265), channel_id=1, source_target_pairs={{0,1},{1,2},{2,3},{3,4},{4,5},{5,6},{6,7},{8,9},{9,10},{10,11},{11... | collective-permute-start | bytes 129032 | tf_op jit(solution)/shard_map/ppermute | solution.py:20
  15.6 0.0 all-reduce.2.cloned.1.call-update
  16.3 0.2 fusion.26
  19.0 0.9 collective-permute-done
  19.9 0.2 pad_maximum_fusion
  20.1 0.3 convolution_add_fusion.1
  20.5 0.2 select_convert_fusion.1
  20.7 0.3 fusion.17
  21.0 0.1 maximum_dynamic-update-slice_fusion.5
  21.2 0.1 maximum_dynamic-update-slice_fusion.3
  21.4 0.1 maximum_dynamic-update-slice_fusion.1
  21.6 1.3 %copy-done.6 = bf16[2,256,2304]{2,1,0:T(8,128)(2,1)S(1)} copy-done((bf16[2,256,2304]{2,1,0:T(8,128)(2,1)S(1)}, bf16[2,256,2304]{2,1,0:T(8,128)(2,1)}, u32[]{:S(2)}) %copy-start.6) | copy-done | bytes 2359320
  22.9 1.1 %fusion.6 = f32[768,256]{1,0:T(8,128)S(1)} fusion(bf16[2304,768]{0,1:T(8,128)(2,1)S(1)} %bitcast.102, bf16[2,256,2304]{2,1,0:T(8,128)(2,1)S(1)} %copy-done.6), kind=kOutput, calls=%fused_computation.10 | convolution fusion | flops 905969664 | bytes 5505024 | tf_op jit(solution)/shard_map/dot_general | solution.py:72
  24.0 0.3 select_convert_fusion.3
  24.3 0.2 fusion.21
  24.5 0.1 maximum_dynamic-update-slice_fusion.17
  24.6 0.1 maximum_dynamic-update-slice_fusion.15
  24.8 0.1 maximum_dynamic-update-slice_fusion.13
  24.9 0.0 copy-start.4
  24.9 0.8 fusion.2
  25.7 0.2 add_convert_fusion.1
  25.9 0.2 fusion.9
  26.2 0.1 mul.139
  26.3 18.9 %all_gather.10 = f32[4,84,4,128]{3,2,1,0:T(4,128)S(1)} all-gather(f32[1,84,4,128]{3,2,1,0:T(4,128)S(1)} %bitcast.99), channel_id=1, replica_groups=mesh['tm'=4,'lat'=8] {'tm'}, dimensions={0}, use_global_device_ids=true | all-gather | bytes 860160 | tf_op jit(solution)/shard_map/all_gather | solution.py:30
  45.2 0.3 while.28
  45.2 0.1 add_select_fusion.4
  45.3 0.1 add_select_fusion.4
  45.4 0.1 add_select_fusion.4
  45.5 7.2 %all-reduce.2.cloned.1.call-done = f32[84,4,128]{2,1,0:T(4,128)} async-done(((f32[84,4,128]{2,1,0:T(4,128)}), f32[84,4,128]{2,1,0:T(4,128)}) %all-reduce.2.cloned.1.call-update) | async-done | bytes 172048 | tf_op jit(solution)/shard_map/psum | solution.py:42
  52.7 1.0 %divide_convert_fusion = (bf16[84,4,128]{2,1,0:T(4,128)(2,1)S(1)}, f32[84,4,128]{2,1,0:T(4,128)S(1)}) fusion(f32[]{:T(128)S(6)} %sqrt.2, f32[84,4,128]{2,1,0:T(4,128)S(1)} %get-tuple-element.163, f32[84,4,128]{2,1,0:T(4,128)} %all-reduce.2.cloned.1.call-done), kind=kLoop, calls=%fused_computation.68 | loop fusion | flops 129024 | bytes 602116 | tf_op jit(solution)/shard_map/convert_element_type | solution.py:105
  53.7 0.1 fusion.23
  53.7 1.9 %collective-permute-start.3 = (bf16[84,2,128]{2,1,0:T(2,128)(2,1)S(1)}, bf16[84,2,128]{2,1,0:T(2,128)(2,1)S(1)}, u32[]{:S(2)}, u32[]{:S(2)}) collective-permute-start(bf16[84,2,128]{2,1,0:T(2,128)(2,1)S(1)} %get-tuple-element.264), channel_id=1, source_target_pairs={{1,0},{2,1},{3,2},{4,3},{5,4},{6,5},{7,6},{9,8},{10,9},{11,10},{12... | collective-permute-start | bytes 129032 | tf_op jit(solution)/shard_map/ppermute | solution.py:23
  55.7 2.4 %collective-permute-start.2 = (bf16[84,2,128]{2,1,0:T(2,128)(2,1)S(1)}, bf16[84,2,128]{2,1,0:T(2,128)(2,1)S(1)}, u32[]{:S(2)}, u32[]{:S(2)}) collective-permute-start(bf16[84,2,128]{2,1,0:T(2,128)(2,1)S(1)} %get-tuple-element.263), channel_id=1, source_target_pairs={{0,1},{1,2},{2,3},{3,4},{4,5},{5,6},{6,7},{8,9},{9,10},{10,11},{11... | collective-permute-start | bytes 129032 | tf_op jit(solution)/shard_map/ppermute | solution.py:20
  58.1 3.8 %collective-permute-done.2 = bf16[84,2,128]{2,1,0:T(2,128)(2,1)S(1)} collective-permute-done((bf16[84,2,128]{2,1,0:T(2,128)(2,1)S(1)}, bf16[84,2,128]{2,1,0:T(2,128)(2,1)S(1)}, u32[]{:S(2)}, u32[]{:S(2)}) %collective-permute-start.2) | collective-permute-done | bytes 43040 | tf_op jit(solution)/shard_map/ppermute | solution.py:20
  61.9 0.2 pad_maximum_fusion.1
  62.1 0.3 convolution_add_fusion
  62.5 0.2 select_convert_fusion
  62.7 0.3 fusion.15
  63.0 0.1 maximum_dynamic-update-slice_fusion.11
  63.2 0.0 copy-start.7
  63.2 0.1 maximum_dynamic-update-slice_fusion.9
  63.4 0.1 maximum_dynamic-update-slice_fusion.7
  63.6 1.3 %copy-done.7 = bf16[2,256,2304]{2,1,0:T(8,128)(2,1)S(1)} copy-done((bf16[2,256,2304]{2,1,0:T(8,128)(2,1)S(1)}, bf16[2,256,2304]{2,1,0:T(8,128)(2,1)}, u32[]{:S(2)}) %copy-start.7) | copy-done | bytes 2359320
  64.9 1.1 %fusion.4 = f32[768,256]{1,0:T(8,128)S(1)} fusion(bf16[2304,768]{0,1:T(8,128)(2,1)S(1)} %bitcast.103, bf16[2,256,2304]{2,1,0:T(8,128)(2,1)S(1)} %copy-done.7), kind=kOutput, calls=%fused_computation.8 | convolution fusion | flops 905969664 | bytes 5505024 | tf_op jit(solution)/shard_map/dot_general | solution.py:72
  66.0 0.3 select_convert_fusion.2
  66.2 0.2 fusion.19
  66.5 0.1 maximum_dynamic-update-slice_fusion.23
  66.6 0.1 maximum_dynamic-update-slice_fusion.21
  66.8 0.1 maximum_dynamic-update-slice_fusion.19
  66.9 0.8 fusion
  67.7 0.2 add_convert_fusion
  67.9 0.2 fusion.8
  68.1 0.1 mul.150
  68.2 17.1 %all-gather = f32[336,4,128]{2,1,0:T(4,128)S(1)} all-gather(f32[84,4,128]{2,1,0:T(4,128)S(1)} %bitcast.85), channel_id=2, replica_groups=mesh['tm'=4,'lat'=8] {'tm'}, dimensions={0}, use_global_device_ids=true | all-gather | bytes 860160 | tf_op jit(solution)/shard_map/all_gather | solution.py:30
  85.4 0.3 while.29
  85.4 0.1 add_select_fusion.5
  85.5 0.1 add_select_fusion.5
  85.6 0.1 add_select_fusion.5
  85.7 0.7 add_bitcast_fusion
  (57 shorter events, 1.0 us)
Async XLA Ops:
  6.5 9.8 %copy-start = (bf16[256,1024]{1,0:T(8,128)(2,1)S(1)}, bf16[256,1024]{1,0:T(8,128)(2,1)}, u32[]{:S(2)}) copy-start(bf16[256,1024]{1,0:T(8,128)(2,1)} %param.16) | copy-start | bytes 1572868
  6.5 13.6 %copy-start.3 = (bf16[256,84]{0,1:T(8,128)(2,1)S(1)}, bf16[256,84]{0,1:T(8,128)(2,1)}, u32[]{:S(2)}) copy-start(bf16[256,84]{0,1:T(8,128)(2,1)} %param.13) | copy-start | bytes 129028
  6.5 13.6 %copy-start.5 = (f32[256]{0:T(256)S(1)}, f32[256]{0:T(256)}, u32[]{:S(2)}) copy-start(f32[256]{0:T(256)} %param.14) | copy-start | bytes 3076
  6.5 46.1 %all-reduce.2.cloned.1.call-start = ((), (), s32[]{:S(2)}) async-start(), calls=%async_computation | async-start | bytes 344064 | tf_op jit(solution)/shard_map/psum | solution.py:42
  10.9 8.2 %collective-permute-start.1 = (bf16[84,2,128]{2,1,0:T(2,128)(2,1)S(1)}, bf16[84,2,128]{2,1,0:T(2,128)(2,1)S(1)}, u32[]{:S(2)}, u32[]{:S(2)}) collective-permute-start(bf16[84,2,128]{2,1,0:T(2,128)(2,1)S(1)} %get-tuple-element.266), channel_id=1, source_target_pairs={{1,0},{2,1},{3,2},{4,3},{5,4},{6,5},{7,6},{9,8},{10,9},{11,10},{12... | collective-permute-start | bytes 129032 | tf_op jit(solution)/shard_map/ppermute | solution.py:23
  13.7 6.2 %collective-permute-start = (bf16[84,2,128]{2,1,0:T(2,128)(2,1)S(1)}, bf16[84,2,128]{2,1,0:T(2,128)(2,1)S(1)}, u32[]{:S(2)}, u32[]{:S(2)}) collective-permute-start(bf16[84,2,128]{2,1,0:T(2,128)(2,1)S(1)} %get-tuple-element.265), channel_id=1, source_target_pairs={{0,1},{1,2},{2,3},{3,4},{4,5},{5,6},{6,7},{8,9},{9,10},{10,11},{11... | collective-permute-start | bytes 129032 | tf_op jit(solution)/shard_map/ppermute | solution.py:20
  21.2 1.7 %copy-start.6 = (bf16[2,256,2304]{2,1,0:T(8,128)(2,1)S(1)}, bf16[2,256,2304]{2,1,0:T(8,128)(2,1)}, u32[]{:S(2)}) copy-start(bf16[2,256,2304]{2,1,0:T(8,128)(2,1)} %param.15) | copy-start | bytes 7077892
  24.9 1.0 %copy-start.4 = (bf16[84,256]{1,0:T(8,128)(2,1)S(1)}, bf16[84,256]{1,0:T(8,128)(2,1)}, u32[]{:S(2)}) copy-start(bf16[84,256]{1,0:T(8,128)(2,1)} %param.17) | copy-start | bytes 129028
  24.9 1.3 %copy-start.1 = (f32[1,84,4,128]{3,2,1,0:T(4,128)S(1)}, f32[1,84,4,128]{3,2,1,0:T(4,128)}, u32[]{:S(2)}) copy-start(f32[1,84,4,128]{3,2,1,0:T(4,128)} %param.11) | copy-start | bytes 516100
  53.7 4.4 %collective-permute-start.3 = (bf16[84,2,128]{2,1,0:T(2,128)(2,1)S(1)}, bf16[84,2,128]{2,1,0:T(2,128)(2,1)S(1)}, u32[]{:S(2)}, u32[]{:S(2)}) collective-permute-start(bf16[84,2,128]{2,1,0:T(2,128)(2,1)S(1)} %get-tuple-element.264), channel_id=1, source_target_pairs={{1,0},{2,1},{3,2},{4,3},{5,4},{6,5},{7,6},{9,8},{10,9},{11,10},{12... | collective-permute-start | bytes 129032 | tf_op jit(solution)/shard_map/ppermute | solution.py:23
  55.7 6.2 %collective-permute-start.2 = (bf16[84,2,128]{2,1,0:T(2,128)(2,1)S(1)}, bf16[84,2,128]{2,1,0:T(2,128)(2,1)S(1)}, u32[]{:S(2)}, u32[]{:S(2)}) collective-permute-start(bf16[84,2,128]{2,1,0:T(2,128)(2,1)S(1)} %get-tuple-element.263), channel_id=1, source_target_pairs={{0,1},{1,2},{2,3},{3,4},{4,5},{5,6},{6,7},{8,9},{9,10},{10,11},{11... | collective-permute-start | bytes 129032 | tf_op jit(solution)/shard_map/ppermute | solution.py:20
  63.2 1.7 %copy-start.7 = (bf16[2,256,2304]{2,1,0:T(8,128)(2,1)S(1)}, bf16[2,256,2304]{2,1,0:T(8,128)(2,1)}, u32[]{:S(2)}) copy-start(bf16[2,256,2304]{2,1,0:T(8,128)(2,1)} %param.15) | copy-start | bytes 7077892
  68.1 17.6 %copy-start.2 = (f32[84,4,128]{2,1,0:T(4,128)S(1)}, f32[84,4,128]{2,1,0:T(4,128)}, u32[]{:S(2)}) copy-start(f32[84,4,128]{2,1,0:T(4,128)} %all-reduce.2.cloned.1.call-done) | copy-start | bytes 516100
Sparse Core Ops, SparseCore 0:
  15.7 36.8 all-reduce.1
where the time goes:
time: 93.6 us; the launch traced here: 93.3 us
  blocking collectives  36 us (38%)
  between operations  18.4 us (20%)
  waiting for transfers between devices  11.9 us (13%)
  starting transfers between devices  9.03 us (10%)
  other arithmetic  7.74 us (8%)
  matrix products  5.12 us (5%)
  local copies, waits for them, and re-layouts  4.94 us (5%)
    all_gather x2, blocking collectives, carried_in(): pieces = lax.all_gather(value, axis)  36 us
    psum x1, waiting for transfers between devices, from_root(): return lax.psum(jnp.where(mine, array, jnp.zeros_like(array)), axis)  7.2 us
    ppermute x2, starting transfers between devices, extended(): lax.ppermute(lax.slice_in_dim(block, 0, width, axis=dim), axis, backward)  4.7 us
    ppermute x2, waiting for transfers between devices, extended(): lax.ppermute(lax.slice_in_dim(block, block.shape[dim] - width, None, axis...  4.67 us
    ppermute x2, starting transfers between devices, extended(): lax.ppermute(lax.slice_in_dim(block, block.shape[dim] - width, None, axis...  4.33 us
    dot_general x4, matrix products, convolve(): response = jnp.dot(weight, flattened, preferred_element_type=jnp.float32)  3.84 us
    unnamed x32, local copies, waits for them, and re-layouts  2.98 us
  transfers between devices with their start and end apart: 5, of which 3 were waited for; matrix products, arithmetic and copies ran while one was open for 6% of the time, Pallas kernels for 0%

commit v1 on v0

v1 whole, which is shorter than its diff:
```python
import functools

import jax
import jax.numpy as jnp
from jax import lax
from jax.experimental import pallas as pl
from jax.experimental.pallas import tpu as pltpu
from jax.sharding import PartitionSpec as P

LEVELS = 64
MESH = pl.DeviceIdType.MESH

sigma_top = 1.0
sigma_low = 0.02
rho_power = 7.0


def level_sigma(level):
    top, low = sigma_top ** (1.0 / rho_power), sigma_low ** (1.0 / rho_power)
    root = top + level.astype(jnp.float32) / (LEVELS - 1) * (low - top)
    square = root * root
    return square * square * square * root


def kernel(
    sizes,
    levels,
    x_hbm,
    in_hbm,
    bias_hbm,
    conv_hbm,
    cond_hbm,
    out_hbm,
    result,
    xs,
    in_w,
    bias_row,
    conv_w,
    cond_w,
    out_w,
    cond,
    bias,
    g_one,
    g_two,
    drift,
    scaled,
    halo_one,
    recv_one,
    send_one,
    halo_two,
    recv_two,
    send_two,
    load_sem,
    halo_one_s,
    halo_one_r,
    chain_one_s,
    chain_one_r,
    halo_two_s,
    halo_two_r,
    chain_two_s,
    chain_two_r,
):
    times, bands, C, R, W, HID = sizes
    pairs = R // 2
    W2 = 2 * W
    padded = scaled.shape[1]
    slot = lax.axis_index("tm")
    band = lax.axis_index("lat")
    has_low, has_high = band > 0, band < bands - 1
    has_next = slot < times - 1

    loads = [
        pltpu.make_async_copy(source, target, load_sem.at[i])
        for i, (source, target) in enumerate(
            [
                (x_hbm, xs.at[pl.ds(0, C * R)]),
                (in_hbm, in_w),
                (bias_hbm, bias_row),
                (cond_hbm, cond_w),
                (conv_hbm.at[0], conv_w.at[0]),
                (conv_hbm.at[1], conv_w.at[1]),
                (out_hbm, out_w),
            ]
        )
    ]
    for load in loads:
        load.start()

    barrier = pltpu.get_barrier_semaphore()

    def greet(axis, index):
        pl.semaphore_signal(barrier, inc=1, device_id={axis: index}, device_id_type=MESH)

    pl.when(has_low)(lambda: greet("lat", band - 1))
    pl.when(has_high)(lambda: greet("lat", band + 1))
    pl.when(slot > 0)(lambda: greet("tm", slot - 1))

    if padded > C:
        xs[C * R :, :] = jnp.zeros((padded * R - C * R, W), jnp.float32)
    drift[...] = jnp.zeros_like(drift)

    sigma = level_sigma(jnp.full((1, W2), levels[slot], jnp.int32))
    sigma_next = level_sigma(jnp.full((1, W2), levels[slot + 1], jnp.int32))
    variance = sigma * sigma + 0.25
    inverse = 1.0 / jnp.sqrt(variance)
    gain = (sigma_next - sigma) / sigma
    keep = gain * (sigma * sigma / variance)
    push = -0.5 * gain * sigma * inverse

    def own(q):
        return jnp.concatenate(
            [xs[pl.ds(2 * q + i, padded, stride=R), :] for i in range(2)], axis=1
        )

    loads[0].wait()
    for q in range(pairs):
        scaled[q] = (own(q) * inverse).astype(jnp.bfloat16)

    def remote(source, target, send, receive, axis, index):
        return pltpu.make_async_remote_copy(
            src_ref=source,
            dst_ref=target,
            send_sem=send,
            recv_sem=receive,
            device_id={axis: index},
            device_id_type=MESH,
        )

    def down(source, halo, send, receive):
        return remote(source, halo.at[1], send.at[1], receive.at[1], "lat", band - 1)

    def up(source, halo, send, receive):
        return remote(source, halo.at[0], send.at[0], receive.at[0], "lat", band + 1)

    def onward(q, source, target, send, receive):
        return remote(
            source.at[q], target.at[q], send.at[q], receive.at[q], "tm", slot + 1
        )

    first = (halo_one, halo_one_s, halo_one_r)
    second = (halo_two, halo_two_s, halo_two_r)
    chain_one = (send_one, recv_one, chain_one_s, chain_one_r)
    chain_two = (send_two, recv_two, chain_two_s, chain_two_r)

    pl.semaphore_wait(
        barrier,
        has_low.astype(jnp.int32) + has_high.astype(jnp.int32) + has_next.astype(jnp.int32),
    )
    pl.when(has_low)(lambda: down(scaled.at[0], *first).start())
    pl.when(has_high)(lambda: up(scaled.at[pairs - 1], *first).start())

    loads[2].wait()
    for j in range(HID // W):
        rows = pl.ds(j * W, W)
        bias[rows, :] = jnp.broadcast_to(bias_row[:, j * W : (j + 1) * W], (W, W)).T

    half = cond_w.shape[0] // 2
    place = lax.broadcasted_iota(jnp.int32, (1, half), 1).astype(jnp.float32) / half
    frequency = jnp.exp(place * jnp.log(jnp.full((1, half), 100.0, jnp.float32)))
    phases = jnp.log(sigma[:, :1]) / 4.0 * frequency
    embedding = jnp.concatenate([jnp.cos(phases), jnp.sin(phases)], axis=1)
    embedding = jnp.broadcast_to(embedding, (W, 2 * half)).astype(jnp.bfloat16)
    loads[3].wait()
    conditions = jnp.dot(embedding, cond_w[...], preferred_element_type=jnp.float32)
    for j in range(4 * HID // W):
        block = conditions[:, j * W : (j + 1) * W].T
        is_scale = (j * W // HID) % 2 == 0
        cond[pl.ds(j * W, W), :] = block + 1.0 if is_scale else block

    def shifts(target, chunk, halves):
        for i, value in enumerate(halves):
            lanes = pl.ds((2 * chunk + i) * W, W)
            target[pl.ds(0, HID), lanes] = pltpu.roll(value, 1, 1).astype(jnp.bfloat16)
            target[pl.ds(HID, HID), lanes] = value.astype(jnp.bfloat16)
            target[pl.ds(2 * HID, HID), lanes] = pltpu.roll(value, W - 1, 1).astype(jnp.bfloat16)

    def project(chunk, value, inside=None):
        hidden = jnp.dot(in_w[...], value, preferred_element_type=jnp.float32)
        halves = []
        for i in range(2):
            part = hidden[:, i * W : (i + 1) * W] + bias[...]
            halves.append(part if inside is None else jnp.where(inside, part, 0.0))
        shifts(g_one, chunk, halves)

    def convolve(source, layer, pair):
        total = None
        for a in range(3):
            term = jnp.dot(
                conv_w[layer, :, a * 3 * HID : (a + 1) * 3 * HID],
                source[:, (2 * pair + a) * W : (2 * pair + a + 2) * W],
                preferred_element_type=jnp.float32,
            )
            total = term if total is None else total + term
        return total

    def activated(response, layer, i):
        scale = cond[pl.ds(2 * layer * HID, HID), :]
        shift = cond[pl.ds((2 * layer + 1) * HID, HID), :]
        value = response[:, i * W : (i + 1) * W] * scale + shift
        part = 0.5 * value
        return part + part * jnp.tanh(part)

    def layer_one(pair):
        response = convolve(g_one, 0, pair)
        halves = [activated(response, 0, i) for i in range(2)]
        if pair == 0:
            halves[0] = jnp.where(has_low, halves[0], 0.0)
        if pair == pairs:
            halves[1] = jnp.where(has_high, halves[1], 0.0)
        shifts(g_two, pair, halves)

    def layer_two(pair, current):
        response = convolve(g_two, 1, pair)
        halves = []
        for i in range(2):
            lanes = pl.ds((2 * pair + 1 + i) * W, W)
            carried = g_two[pl.ds(HID, HID), lanes].astype(jnp.float32)
            halves.append((carried + activated(response, 1, i)).astype(jnp.bfloat16))
        network = jnp.dot(
            out_w[...], jnp.concatenate(halves, axis=1), preferred_element_type=jnp.float32
        )
        drift[pair, 0:C, :] = push * network
        return keep * current + drift[pair]

    def write(pair, value):
        for i in range(2):
            result[pl.ds(2 * pair + i, C, stride=R), :] = value[0:C, i * W : (i + 1) * W]

    loads[1].wait()
    for q in range(pairs):
        project(q + 1, scaled[q, 0:C, :])
    loads[4].wait()
    for pair in range(1, pairs):
        layer_one(pair)
    pl.when(has_low)(lambda: up(scaled.at[pairs - 1], *first).wait_recv())
    project(0, halo_one[0, 0:C, :], has_low)
    layer_one(0)
    loads[5].wait()
    loads[6].wait()
    for q in range(pairs):
        if q == pairs - 1:
            pl.when(has_high)(lambda: down(scaled.at[0], *first).wait_recv())
            project(pairs + 1, halo_one[1, 0:C, :], has_high)
            layer_one(pairs)
        current = own(q)
        change = layer_two(q, current)

        @pl.when(slot == 0)
        def _():
            total = current + change
            write(q, total)
            send_one[q] = total.astype(jnp.bfloat16)

        @pl.when(slot > 0)
        def _():
            onward(q, *chain_one).wait_recv()
            if q == 0:
                pl.when(has_low)(lambda: down(recv_one.at[0], *second).start())
            if q == pairs - 1:
                pl.when(has_high)(lambda: up(recv_one.at[pairs - 1], *second).start())
            send_one[q] = (recv_one[q].astype(jnp.float32) + change).astype(jnp.bfloat16)

        pl.when(has_next)(lambda: onward(q, *chain_one).start())

    @pl.when(slot > 0)
    def _():
        def state(q):
            return recv_one[q].astype(jnp.float32)

        def rescaled(value):
            return (value[0:C].astype(jnp.float32) * inverse).astype(jnp.bfloat16)

        for q in range(pairs):
            project(q + 1, rescaled(recv_one[q]))
        for pair in range(1, pairs):
            layer_one(pair)
        pl.when(has_high)(lambda: down(recv_one.at[0], *second).wait_recv())
        project(pairs + 1, rescaled(halo_two[1]), has_high)
        layer_one(pairs)
        for q in reversed(range(pairs)):
            if q == 0:
                pl.when(has_low)(lambda: up(recv_one.at[pairs - 1], *second).wait_recv())
                project(0, rescaled(halo_two[0]), has_low)
                layer_one(0)
            current = state(q)
            change = layer_two(q, current)

            @pl.when(slot == 1)
            def _():
                total = current + change
                write(q, total)
                send_two[q] = total.astype(jnp.bfloat16)

            @pl.when(slot > 1)
            def _():
                onward(q, *chain_two).wait_recv()
                total = recv_two[q].astype(jnp.float32) + change
                write(q, total)
                send_two[q] = total.astype(jnp.bfloat16)

            pl.when(has_next)(lambda: onward(q, *chain_two).start())

    pl.when(has_low)(lambda: down(scaled.at[0], *first).wait_send())
    pl.when(has_high)(lambda: up(scaled.at[pairs - 1], *first).wait_send())

    @pl.when(has_next)
    def _():
        for q in range(pairs):
            onward(q, *chain_one).wait_send()

    @pl.when(slot > 0)
    def _():
        pl.when(has_low)(lambda: down(recv_one.at[0], *second).wait_send())
        pl.when(has_high)(lambda: up(recv_one.at[pairs - 1], *second).wait_send())

        @pl.when(has_next)
        def _():
            for q in range(pairs):
                onward(q, *chain_two).wait_send()


def on_device(times, bands, trajectory, step_levels, in_weight, in_bias, conv_weight, cond_weight, out_weight):
    _, C, R, W = trajectory.shape
    HID = in_weight.shape[0]
    pairs = R // 2
    padded = -(-C // 16) * 16
    bf16, f32 = jnp.bfloat16, jnp.float32
    block = (pairs, padded, 2 * W)
    halo = (2, padded, 2 * W)
    anywhere = pl.BlockSpec(memory_space=pl.ANY)
    dma = pltpu.SemaphoreType.DMA
    result = pl.pallas_call(
        functools.partial(kernel, (times, bands, C, R, W, HID)),
        out_shape=jax.ShapeDtypeStruct((C * R, W), f32),
        in_specs=[pl.BlockSpec(memory_space=pltpu.SMEM)] + [anywhere] * 6,
        out_specs=pl.BlockSpec(memory_space=pltpu.VMEM),
        scratch_shapes=[
            pltpu.VMEM((padded * R, W), f32),
            pltpu.VMEM(in_weight.shape, bf16),
            pltpu.VMEM((1, HID), f32),
            pltpu.VMEM(conv_weight.shape, bf16),
            pltpu.VMEM(cond_weight.shape, bf16),
            pltpu.VMEM(out_weight.shape, bf16),
            pltpu.VMEM((4 * HID, W), f32),
            pltpu.VMEM((HID, W), f32),
            pltpu.VMEM((3 * HID, (R + 4) * W), bf16),
            pltpu.VMEM((3 * HID, (R + 2) * W), bf16),
            pltpu.VMEM(block, f32),
            pltpu.VMEM(block, bf16),
            pltpu.VMEM(halo, bf16),
            pltpu.VMEM(block, bf16),
            pltpu.VMEM(block, bf16),
            pltpu.VMEM(halo, bf16),
            pltpu.VMEM(block, bf16),
            pltpu.VMEM(block, bf16),
            dma((7,)),
            dma((2,)),
            dma((2,)),
            dma((pairs,)),
            dma((pairs,)),
            dma((2,)),
            dma((2,)),
            dma((pairs,)),
            dma((pairs,)),
        ],
        compiler_params=pltpu.CompilerParams(
            collective_id=0, has_side_effects=True, vmem_limit_bytes=32 * 1024 * 1024
        ),
    )(
        step_levels,
        trajectory.reshape(C * R, W),
        in_weight,
        in_bias.reshape(1, HID),
        conv_weight,
        cond_weight,
        out_weight,
    )
    return result.reshape(1, C, R, W)


def solution(mesh):
    in_specs = (P("tm", None, "lat", None), P(), P(), P(), P(), P(), P())
    out_specs = P("tm", None, "lat", None)
    return jax.shard_map(
        functools.partial(on_device, mesh.shape["tm"], mesh.shape["lat"]),
        mesh=mesh,
        in_specs=in_specs,
        out_specs=out_specs,
        check_vma=False,
    )
```

time: 93.6 us -> 31.5 us (0.34)
  the two profiles are of different devices: /device:TPU:4 before, /device:TPU:27 now
where the time goes in v1:
time: 31.5 us; the launch traced here: 31.1 us
  Pallas kernels  23.8 us (76%)
  local copies, waits for them, and re-layouts  7.33 us (23%)
    pallas_call x1, Pallas kernels, on_device(): pl.pallas_call(functools.partial(kernel, (times, bands, C, R, W, HID)), o...  23.8 us
    unnamed x14, local copies, waits for them, and re-layouts  7.33 us

profile of v1, /device:TPU:27, one launch (start us, length us, event | category | flops | bytes accessed | tf_op | source)
XLA Modules:
  0.0 31.1 jit_solution(6390362920667326320)
XLA Ops:
  0.0 0.9 %copy.8.in_hbm = bf16[256,84]{1,0:T(8,128)(2,1)S(1)} copy(bf16[256,84]{0,1:T(8,128)(2,1)} %param.9) | data formatting | bytes 86016 | tf_op args[2]
  0.9 0.0 copy-start
  0.9 1.7 %copy-done = bf16[2,256,2304]{2,1,0:T(8,128)(2,1)S(1)} copy-done((bf16[2,256,2304]{2,1,0:T(8,128)(2,1)S(1)}, bf16[2,256,2304]{2,1,0:T(8,128)(2,1)}, u32[]{:S(2)}) %copy-start) | copy-done | bytes 2359320
  2.6 0.0 copy-start.1
  2.6 1.0 %copy-done.1 = bf16[256,1024]{1,0:T(8,128)(2,1)S(1)} copy-done((bf16[256,1024]{1,0:T(8,128)(2,1)S(1)}, bf16[256,1024]{1,0:T(8,128)(2,1)}, u32[]{:S(2)}) %copy-start.1) | copy-done | bytes 524312
  3.6 0.0 copy-start.2
  3.6 0.9 %copy-done.2 = f32[1,84,4,128]{3,2,1,0:T(4,128)S(1)} copy-done((f32[1,84,4,128]{3,2,1,0:T(4,128)S(1)}, f32[1,84,4,128]{3,2,1,0:T(4,128)}, u32[]{:S(2)}) %copy-start.2) | copy-done | bytes 172056
  4.5 0.0 copy-start.3
  4.5 0.8 %copy-done.3 = bf16[84,256]{1,0:T(8,128)(2,1)S(1)} copy-done((bf16[84,256]{1,0:T(8,128)(2,1)S(1)}, bf16[84,256]{1,0:T(8,128)(2,1)}, u32[]{:S(2)}) %copy-start.3) | copy-done | bytes 43032
  5.3 0.0 copy-start.4
  5.3 0.7 %copy-done.4 = f32[256]{0:T(256)S(1)} copy-done((f32[256]{0:T(256)S(1)}, f32[256]{0:T(256)}, u32[]{:S(2)}) %copy-start.4) | copy-done | bytes 1048
  6.0 0.0 copy-start.5
  6.0 0.7 %copy-done.5 = s32[5]{0:T(128)S(1)} copy-done((s32[5]{0:T(128)S(1)}, s32[5]{0:T(128)}, u32[]{:S(2)}) %copy-start.5) | copy-done | bytes 44
  6.7 23.8 %shard_map.73 = f32[336,128]{1,0:T(8,128)S(1)} custom-call(s32[5]{0:T(128)S(1)} %copy-done.5, f32[336,128]{1,0:T(8,128)S(1)} %bitcast.4, bf16[256,84]{1,0:T(8,128)(2,1)S(1)} %copy.8.in_hbm, f32[1,256]{1,0:T(1,128)S(1)} %bitcast.5, bf16[2,256,2304]{2,1,0:T(8,128)(2,1)S(1)} %copy-done, bf16[256,1024]{1,0:T(8,128)(2,1)S(1)} %copy-done.1, ...), custom_call_target="tpu_custom_call" | custom-call | tf_op jit(solution)/shard_map/pallas_call | solution.py:332
  30.4 0.7 %copy.10 = f32[1,84,4,128]{3,2,1,0:T(4,128)} copy(f32[1,84,4,128]{3,2,1,0:T(4,128)S(1)} %bitcast.3) | data formatting | bytes 344064
Async XLA Ops:
  0.9 1.7 %copy-start = (bf16[2,256,2304]{2,1,0:T(8,128)(2,1)S(1)}, bf16[2,256,2304]{2,1,0:T(8,128)(2,1)}, u32[]{:S(2)}) copy-start(bf16[2,256,2304]{2,1,0:T(8,128)(2,1)} %conv_hbm.1) | copy-start | bytes 7077892
  2.6 1.0 %copy-start.1 = (bf16[256,1024]{1,0:T(8,128)(2,1)S(1)}, bf16[256,1024]{1,0:T(8,128)(2,1)}, u32[]{:S(2)}) copy-start(bf16[256,1024]{1,0:T(8,128)(2,1)} %cond_hbm.1) | copy-start | bytes 1572868
  3.6 0.9 %copy-start.2 = (f32[1,84,4,128]{3,2,1,0:T(4,128)S(1)}, f32[1,84,4,128]{3,2,1,0:T(4,128)}, u32[]{:S(2)}) copy-start(f32[1,84,4,128]{3,2,1,0:T(4,128)} %param.7) | copy-start | bytes 516100
  4.5 0.8 %copy-start.3 = (bf16[84,256]{1,0:T(8,128)(2,1)S(1)}, bf16[84,256]{1,0:T(8,128)(2,1)}, u32[]{:S(2)}) copy-start(bf16[84,256]{1,0:T(8,128)(2,1)} %out_hbm.1) | copy-start | bytes 129028
  5.3 0.7 %copy-start.4 = (f32[256]{0:T(256)S(1)}, f32[256]{0:T(256)}, u32[]{:S(2)}) copy-start(f32[256]{0:T(256)} %param.10) | copy-start | bytes 3076
  6.0 0.7 %copy-start.5 = (s32[5]{0:T(128)S(1)}, s32[5]{0:T(128)}, u32[]{:S(2)}) copy-start(s32[5]{0:T(128)} %levels.1) | copy-start | bytes 64

commit v2 on v1

--- a/solution.py
+++ b/solution.py
@@ -33,6 +33,8 @@
     out_hbm,
     result,
     xs,
+    in_t,
+    in_pad,
     in_w,
     bias_row,
     conv_w,
@@ -74,7 +76,7 @@
         for i, (source, target) in enumerate(
             [
                 (x_hbm, xs.at[pl.ds(0, C * R)]),
-                (in_hbm, in_w),
+                (in_hbm, in_t),
                 (bias_hbm, bias_row),
                 (cond_hbm, cond_w),
                 (conv_hbm.at[0], conv_w.at[0]),
@@ -149,9 +151,13 @@
     pl.when(has_low)(lambda: down(scaled.at[0], *first).start())
     pl.when(has_high)(lambda: up(scaled.at[pairs - 1], *first).start())
 
+    in_pad[...] = jnp.zeros_like(in_pad)
+    loads[1].wait()
     loads[2].wait()
+    in_pad[0:C, :] = in_t[...].astype(jnp.float32)
     for j in range(HID // W):
         rows = pl.ds(j * W, W)
+        in_w[rows, :] = in_pad[:, j * W : (j + 1) * W].T.astype(jnp.bfloat16)
         bias[rows, :] = jnp.broadcast_to(bias_row[:, j * W : (j + 1) * W], (W, W)).T
 
     half = cond_w.shape[0] // 2
@@ -175,7 +181,7 @@
             target[pl.ds(2 * HID, HID), lanes] = pltpu.roll(value, W - 1, 1).astype(jnp.bfloat16)
 
     def project(chunk, value, inside=None):
-        hidden = jnp.dot(in_w[...], value, preferred_element_type=jnp.float32)
+        hidden = jnp.dot(in_w[:, :padded], value, preferred_element_type=jnp.float32)
         halves = []
         for i in range(2):
             part = hidden[:, i * W : (i + 1) * W] + bias[...]
@@ -226,21 +232,20 @@
         for i in range(2):
             result[pl.ds(2 * pair + i, C, stride=R), :] = value[0:C, i * W : (i + 1) * W]
 
-    loads[1].wait()
     for q in range(pairs):
-        project(q + 1, scaled[q, 0:C, :])
+        project(q + 1, scaled[q])
     loads[4].wait()
     for pair in range(1, pairs):
         layer_one(pair)
     pl.when(has_low)(lambda: up(scaled.at[pairs - 1], *first).wait_recv())
-    project(0, halo_one[0, 0:C, :], has_low)
+    project(0, halo_one[0], has_low)
     layer_one(0)
     loads[5].wait()
     loads[6].wait()
     for q in range(pairs):
         if q == pairs - 1:
             pl.when(has_high)(lambda: down(scaled.at[0], *first).wait_recv())
-            project(pairs + 1, halo_one[1, 0:C, :], has_high)
+            project(pairs + 1, halo_one[1], has_high)
             layer_one(pairs)
         current = own(q)
         change = layer_two(q, current)
@@ -268,7 +273,7 @@
             return recv_one[q].astype(jnp.float32)
 
         def rescaled(value):
-            return (value[0:C].astype(jnp.float32) * inverse).astype(jnp.bfloat16)
+            return (value.astype(jnp.float32) * inverse).astype(jnp.bfloat16)
 
         for q in range(pairs):
             project(q + 1, rescaled(recv_one[q]))
@@ -324,10 +329,11 @@
     HID = in_weight.shape[0]
     pairs = R // 2
     padded = -(-C // 16) * 16
+    wide = -(-C // 128) * 128
     bf16, f32 = jnp.bfloat16, jnp.float32
     block = (pairs, padded, 2 * W)
     halo = (2, padded, 2 * W)
-    anywhere = pl.BlockSpec(memory_space=pl.ANY)
+    anywhere = pl.BlockSpec(memory_space=pltpu.HBM)
     dma = pltpu.SemaphoreType.DMA
     result = pl.pallas_call(
         functools.partial(kernel, (times, bands, C, R, W, HID)),
@@ -336,7 +342,9 @@
         out_specs=pl.BlockSpec(memory_space=pltpu.VMEM),
         scratch_shapes=[
             pltpu.VMEM((padded * R, W), f32),
-            pltpu.VMEM(in_weight.shape, bf16),
+            pltpu.VMEM((C, HID), bf16),
+            pltpu.VMEM((wide, HID), f32),
+            pltpu.VMEM((HID, wide), bf16),
             pltpu.VMEM((1, HID), f32),
             pltpu.VMEM(conv_weight.shape, bf16),
             pltpu.VMEM(cond_weight.shape, bf16),
@@ -364,12 +372,12 @@
             dma((pairs,)),
         ],
         compiler_params=pltpu.CompilerParams(
-            collective_id=0, has_side_effects=True, vmem_limit_bytes=32 * 1024 * 1024
+            collective_id=0, has_side_effects=True, vmem_limit_bytes=60 * 1024 * 1024
         ),
     )(
         step_levels,
         trajectory.reshape(C * R, W),
-        in_weight,
+        in_weight.T,
         in_bias.reshape(1, HID),
         conv_weight,
         cond_weight,

time: 31.5 us -> 25.4 us (0.81)
  local copies, waits for them, and re-layouts: 7.33 us -> 1.6 us
    unnamed x14 -> x1, local copies, waits for them, and re-layouts: 7.33 us -> 1.6 us
where the time goes in v2:
time: 25.4 us; the launch traced here: 25.3 us
  Pallas kernels  23.7 us (93%)
  local copies, waits for them, and re-layouts  1.6 us (6%)
    pallas_call x1, Pallas kernels, on_device(): pl.pallas_call(functools.partial(kernel, (times, bands, C, R, W, HID)), o...  23.7 us
    unnamed x1, local copies, waits for them, and re-layouts  1.6 us

profile of v2, /device:TPU:27, one launch (start us, length us, event | category | flops | bytes accessed | tf_op | source)
XLA Modules:
  0.0 25.3 jit_solution(98613362262149904)
XLA Ops:
  0.0 23.7 %shard_map.73 = f32[336,128]{1,0:T(8,128)} custom-call(s32[5]{0:T(128)} %levels.1, f32[336,128]{1,0:T(8,128)} %bitcast.5, bf16[84,256]{1,0:T(8,128)(2,1)} %bitcast.6, f32[1,256]{1,0:T(1,128)} %bitcast.7, bf16[2,256,2304]{2,1,0:T(8,128)(2,1)} %conv_hbm.1, bf16[256,1024]{1,0:T(8,128)(2,1)} %cond_hbm.1, bf16[84,256]{1,0:T(8,128)(2,1)} %out_hbm.1), custom_call_target="tpu_custom_call" | custom-call | tf_op jit(solution)/shard_map/pallas_call | solution.py:338
  23.7 1.6 %copy.9 = f32[1,84,4,128]{3,2,1,0:T(4,128)} copy(f32[1,84,4,128]{3,2,1,0:T(4,128)} %bitcast.4) | data formatting | bytes 344064

commit v3 on v2

--- a/solution.py
+++ b/solution.py
@@ -24,7 +24,7 @@
 
 def kernel(
     sizes,
-    levels,
+    levels_hbm,
     x_hbm,
     in_hbm,
     bias_hbm,
@@ -32,6 +32,7 @@
     cond_hbm,
     out_hbm,
     result,
+    levels,
     xs,
     in_t,
     in_pad,
@@ -82,10 +83,11 @@
                 (conv_hbm.at[0], conv_w.at[0]),
                 (conv_hbm.at[1], conv_w.at[1]),
                 (out_hbm, out_w),
+                (levels_hbm, levels),
             ]
         )
     ]
-    for load in loads:
+    for load in loads[-1:] + loads[:-1]:
         load.start()
 
     barrier = pltpu.get_barrier_semaphore()
@@ -101,6 +103,7 @@
         xs[C * R :, :] = jnp.zeros((padded * R - C * R, W), jnp.float32)
     drift[...] = jnp.zeros_like(drift)
 
+    loads[7].wait()
     sigma = level_sigma(jnp.full((1, W2), levels[slot], jnp.int32))
     sigma_next = level_sigma(jnp.full((1, W2), levels[slot + 1], jnp.int32))
     variance = sigma * sigma + 0.25
@@ -189,15 +192,10 @@
         shifts(g_one, chunk, halves)
 
     def convolve(source, layer, pair):
-        total = None
-        for a in range(3):
-            term = jnp.dot(
-                conv_w[layer, :, a * 3 * HID : (a + 1) * 3 * HID],
-                source[:, (2 * pair + a) * W : (2 * pair + a + 2) * W],
-                preferred_element_type=jnp.float32,
-            )
-            total = term if total is None else total + term
-        return total
+        rows = [source[:, (2 * pair + a) * W : (2 * pair + a + 2) * W] for a in range(3)]
+        return jnp.dot(
+            conv_w[layer], jnp.concatenate(rows, axis=0), preferred_element_type=jnp.float32
+        )
 
     def activated(response, layer, i):
         scale = cond[pl.ds(2 * layer * HID, HID), :]
@@ -206,8 +204,7 @@
         part = 0.5 * value
         return part + part * jnp.tanh(part)
 
-    def layer_one(pair):
-        response = convolve(g_one, 0, pair)
+    def after_one(pair, response):
         halves = [activated(response, 0, i) for i in range(2)]
         if pair == 0:
             halves[0] = jnp.where(has_low, halves[0], 0.0)
@@ -215,8 +212,7 @@
             halves[1] = jnp.where(has_high, halves[1], 0.0)
         shifts(g_two, pair, halves)
 
-    def layer_two(pair, current):
-        response = convolve(g_two, 1, pair)
+    def after_two(pair, response, current):
         halves = []
         for i in range(2):
             lanes = pl.ds((2 * pair + 1 + i) * W, W)
@@ -228,31 +224,43 @@
         drift[pair, 0:C, :] = push * network
         return keep * current + drift[pair]
 
+    def inner(values):
+        for q, value in enumerate(values):
+            project(q + 1, value)
+        responses = [convolve(g_one, 0, pair) for pair in range(1, pairs)]
+        for pair, response in enumerate(responses):
+            after_one(pair + 1, response)
+
+    def outer(low, high):
+        project(0, low, has_low)
+        project(pairs + 1, high, has_high)
+        responses = [convolve(g_one, 0, pair) for pair in (0, pairs)]
+        for pair, response in zip((0, pairs), responses):
+            after_one(pair, response)
+
+    def changes(current):
+        response = convolve(g_two, 1, 0)
+        for q in range(pairs):
+            later = convolve(g_two, 1, q + 1) if q + 1 < pairs else None
+            yield q, after_two(q, response, current(q))
+            response = later
+
     def write(pair, value):
         for i in range(2):
             result[pl.ds(2 * pair + i, C, stride=R), :] = value[0:C, i * W : (i + 1) * W]
 
-    for q in range(pairs):
-        project(q + 1, scaled[q])
     loads[4].wait()
-    for pair in range(1, pairs):
-        layer_one(pair)
-    pl.when(has_low)(lambda: up(scaled.at[pairs - 1], *first).wait_recv())
-    project(0, halo_one[0], has_low)
-    layer_one(0)
+    inner([scaled[q] for q in range(pairs)])
     loads[5].wait()
     loads[6].wait()
-    for q in range(pairs):
-        if q == pairs - 1:
-            pl.when(has_high)(lambda: down(scaled.at[0], *first).wait_recv())
-            project(pairs + 1, halo_one[1], has_high)
-            layer_one(pairs)
-        current = own(q)
-        change = layer_two(q, current)
+    pl.when(has_low)(lambda: up(scaled.at[pairs - 1], *first).wait_recv())
+    pl.when(has_high)(lambda: down(scaled.at[0], *first).wait_recv())
+    outer(halo_one[0], halo_one[1])
+    for q, change in changes(own):
 
         @pl.when(slot == 0)
         def _():
-            total = current + change
+            total = own(q) + change
             write(q, total)
             send_one[q] = total.astype(jnp.bfloat16)
 
@@ -275,24 +283,15 @@
         def rescaled(value):
             return (value.astype(jnp.float32) * inverse).astype(jnp.bfloat16)
 
-        for q in range(pairs):
-            project(q + 1, rescaled(recv_one[q]))
-        for pair in range(1, pairs):
-            layer_one(pair)
+        inner([rescaled(recv_one[q]) for q in range(pairs)])
         pl.when(has_high)(lambda: down(recv_one.at[0], *second).wait_recv())
-        project(pairs + 1, rescaled(halo_two[1]), has_high)
-        layer_one(pairs)
-        for q in reversed(range(pairs)):
-            if q == 0:
-                pl.when(has_low)(lambda: up(recv_one.at[pairs - 1], *second).wait_recv())
-                project(0, rescaled(halo_two[0]), has_low)
-                layer_one(0)
-            current = state(q)
-            change = layer_two(q, current)
+        pl.when(has_low)(lambda: up(recv_one.at[pairs - 1], *second).wait_recv())
+        outer(rescaled(halo_two[0]), rescaled(halo_two[1]))
+        for q, change in changes(state):
 
             @pl.when(slot == 1)
             def _():
-                total = current + change
+                total = state(q) + change
                 write(q, total)
                 send_two[q] = total.astype(jnp.bfloat16)
 
@@ -338,9 +337,10 @@
     result = pl.pallas_call(
         functools.partial(kernel, (times, bands, C, R, W, HID)),
         out_shape=jax.ShapeDtypeStruct((C * R, W), f32),
-        in_specs=[pl.BlockSpec(memory_space=pltpu.SMEM)] + [anywhere] * 6,
+        in_specs=[anywhere] * 7,
         out_specs=pl.BlockSpec(memory_space=pltpu.VMEM),
         scratch_shapes=[
+            pltpu.SMEM(step_levels.shape, jnp.int32),
             pltpu.VMEM((padded * R, W), f32),
             pltpu.VMEM((C, HID), bf16),
             pltpu.VMEM((wide, HID), f32),
@@ -361,7 +361,7 @@
             pltpu.VMEM(halo, bf16),
             pltpu.VMEM(block, bf16),
             pltpu.VMEM(block, bf16),
-            dma((7,)),
+            dma((8,)),
             dma((2,)),
             dma((2,)),
             dma((pairs,)),
@@ -372,16 +372,21 @@
             dma((pairs,)),
         ],
         compiler_params=pltpu.CompilerParams(
-            collective_id=0, has_side_effects=True, vmem_limit_bytes=60 * 1024 * 1024
+            collective_id=0, has_side_effects=True, vmem_limit_bytes=32 * 1024 * 1024
         ),
     )(
-        step_levels,
-        trajectory.reshape(C * R, W),
-        in_weight.T,
-        in_bias.reshape(1, HID),
-        conv_weight,
-        cond_weight,
-        out_weight,
+        *(
+            pltpu.with_memory_space_constraint(operand, pltpu.HBM)
+            for operand in (
+                step_levels,
+                trajectory.reshape(C * R, W),
+                in_weight.T,
+                in_bias.reshape(1, HID),
+                conv_weight,
+                cond_weight,
+                out_weight,
+            )
+        ),
     )
     return result.reshape(1, C, R, W)
 

time: 25.4 us -> 22.2 us (0.87)
  Pallas kernels: 23.7 us -> 21.4 us
  local copies, waits for them, and re-layouts: 1.6 us -> 0.67 us
    pallas_call x1, Pallas kernels: 23.7 us -> 21.4 us  [on_device(): pl.pallas_call(functools.partial(kernel, (times, bands, C, R, W, HID)), o...]
    unnamed x1, local copies, waits for them, and re-layouts: 1.6 us -> 0.67 us
where the time goes in v3:
time: 22.2 us; the launch traced here: 22.1 us
  Pallas kernels  21.4 us (96%)
  local copies, waits for them, and re-layouts  0.67 us (3%)
    pallas_call x1, Pallas kernels, on_device(): pl.pallas_call(functools.partial(kernel, (times, bands, C, R, W, HID)), o...  21.4 us
    unnamed x1, local copies, waits for them, and re-layouts  0.67 us

profile of v3, /device:TPU:27, one launch (start us, length us, event | category | flops | bytes accessed | tf_op | source)
XLA Modules:
  0.0 22.1 jit_solution(6061383828516207092)
XLA Ops:
  0.0 21.4 %shard_map.73 = f32[336,128]{1,0:T(8,128)S(1)} custom-call(s32[5]{0:T(128)} %levels_hbm.1, f32[336,128]{1,0:T(8,128)} %bitcast.5, bf16[84,256]{1,0:T(8,128)(2,1)} %bitcast.6, f32[1,256]{1,0:T(1,128)} %bitcast.7, bf16[2,256,2304]{2,1,0:T(8,128)(2,1)} %conv_hbm.1, bf16[256,1024]{1,0:T(8,128)(2,1)} %cond_hbm.1, bf16[84,256]{1,0:T(8,128)(2,1)} %out_hbm.1), custom_call_target="tpu_custom_call" | custom-call | tf_op jit(solution)/shard_map/pallas_call | solution.py:337
  21.4 0.7 %copy.9 = f32[1,84,4,128]{3,2,1,0:T(4,128)} copy(f32[1,84,4,128]{3,2,1,0:T(4,128)S(1)} %bitcast.4) | data formatting | bytes 344064

commit v4 on v3

--- a/solution.py
+++ b/solution.py
@@ -177,25 +177,37 @@
         cond[pl.ds(j * W, W), :] = block + 1.0 if is_scale else block
 
     def shifts(target, chunk, halves):
-        for i, value in enumerate(halves):
+        for i, half in enumerate(halves):
             lanes = pl.ds((2 * chunk + i) * W, W)
-            target[pl.ds(0, HID), lanes] = pltpu.roll(value, 1, 1).astype(jnp.bfloat16)
-            target[pl.ds(HID, HID), lanes] = value.astype(jnp.bfloat16)
-            target[pl.ds(2 * HID, HID), lanes] = pltpu.roll(value, W - 1, 1).astype(jnp.bfloat16)
-
-    def project(chunk, value, inside=None):
-        hidden = jnp.dot(in_w[:, :padded], value, preferred_element_type=jnp.float32)
-        halves = []
-        for i in range(2):
-            part = hidden[:, i * W : (i + 1) * W] + bias[...]
-            halves.append(part if inside is None else jnp.where(inside, part, 0.0))
-        shifts(g_one, chunk, halves)
-
-    def convolve(source, layer, pair):
-        rows = [source[:, (2 * pair + a) * W : (2 * pair + a + 2) * W] for a in range(3)]
-        return jnp.dot(
+            value = half.astype(jnp.bfloat16)
+            target[pl.ds(0, HID), lanes] = pltpu.roll(value, 1, 1)
+            target[pl.ds(HID, HID), lanes] = value
+            target[pl.ds(2 * HID, HID), lanes] = pltpu.roll(value, W - 1, 1)
+
+    def project(chunks, values, insides=None):
+        hidden = jnp.dot(
+            in_w[:, :padded],
+            jnp.concatenate(values, axis=1),
+            preferred_element_type=jnp.float32,
+        )
+        for j, chunk in enumerate(chunks):
+            halves = []
+            for i in range(2):
+                part = hidden[:, (2 * j + i) * W : (2 * j + i + 1) * W] + bias[...]
+                halves.append(part if insides is None else jnp.where(insides[j], part, 0.0))
+            shifts(g_one, chunk, halves)
+
+    def convolve(source, layer, firsts):
+        rows = [
+            jnp.concatenate(
+                [source[:, (2 * pair + a) * W : (2 * pair + a + 2) * W] for pair in firsts], axis=1
+            )
+            for a in range(3)
+        ]
+        response = jnp.dot(
             conv_w[layer], jnp.concatenate(rows, axis=0), preferred_element_type=jnp.float32
         )
+        return [response[:, j * W2 : (j + 1) * W2] for j in range(len(firsts))]
 
     def activated(response, layer, i):
         scale = cond[pl.ds(2 * layer * HID, HID), :]
@@ -212,38 +224,32 @@
             halves[1] = jnp.where(has_high, halves[1], 0.0)
         shifts(g_two, pair, halves)
 
-    def after_two(pair, response, current):
+    def inner(values):
+        project(range(1, pairs + 1), values)
+        middle = range(1, pairs)
+        if middle:
+            for pair, response in zip(middle, convolve(g_one, 0, middle)):
+                after_one(pair, response)
+
+    def outer(low, high):
+        project((0, pairs + 1), (low, high), (has_low, has_high))
+        for pair, response in zip((0, pairs), convolve(g_one, 0, (0, pairs))):
+            after_one(pair, response)
+
+    def changes(current):
         halves = []
-        for i in range(2):
-            lanes = pl.ds((2 * pair + 1 + i) * W, W)
-            carried = g_two[pl.ds(HID, HID), lanes].astype(jnp.float32)
-            halves.append((carried + activated(response, 1, i)).astype(jnp.bfloat16))
+        for q, response in enumerate(convolve(g_two, 1, range(pairs))):
+            for i in range(2):
+                lanes = pl.ds((2 * q + 1 + i) * W, W)
+                carried = g_two[pl.ds(HID, HID), lanes].astype(jnp.float32)
+                halves.append((carried + activated(response, 1, i)).astype(jnp.bfloat16))
         network = jnp.dot(
             out_w[...], jnp.concatenate(halves, axis=1), preferred_element_type=jnp.float32
         )
-        drift[pair, 0:C, :] = push * network
-        return keep * current + drift[pair]
-
-    def inner(values):
-        for q, value in enumerate(values):
-            project(q + 1, value)
-        responses = [convolve(g_one, 0, pair) for pair in range(1, pairs)]
-        for pair, response in enumerate(responses):
-            after_one(pair + 1, response)
-
-    def outer(low, high):
-        project(0, low, has_low)
-        project(pairs + 1, high, has_high)
-        responses = [convolve(g_one, 0, pair) for pair in (0, pairs)]
-        for pair, response in zip((0, pairs), responses):
-            after_one(pair, response)
-
-    def changes(current):
-        response = convolve(g_two, 1, 0)
         for q in range(pairs):
-            later = convolve(g_two, 1, q + 1) if q + 1 < pairs else None
-            yield q, after_two(q, response, current(q))
-            response = later
+            drift[q, 0:C, :] = push * network[:, q * W2 : (q + 1) * W2]
+        for q in range(pairs):
+            yield q, keep * current(q) + drift[q]
 
     def write(pair, value):
         for i in range(2):

time: 22.2 us -> 22 us (level)
  no operation moved by 1% of the time
where the time goes in v4:
time: 22 us; the launch traced here: 21.9 us
  Pallas kernels  21.2 us (96%)
  local copies, waits for them, and re-layouts  0.67 us (3%)
    pallas_call x1, Pallas kernels, on_device(): pl.pallas_call(functools.partial(kernel, (times, bands, C, R, W, HID)), o...  21.2 us
    unnamed x1, local copies, waits for them, and re-layouts  0.67 us

profile of v4, /device:TPU:27, one launch (start us, length us, event | category | flops | bytes accessed | tf_op | source)
XLA Modules:
  0.0 21.9 jit_solution(10670656684458593052)
XLA Ops:
  0.0 21.2 %shard_map.73 = f32[336,128]{1,0:T(8,128)S(1)} custom-call(s32[5]{0:T(128)} %levels_hbm.1, f32[336,128]{1,0:T(8,128)} %bitcast.5, bf16[84,256]{1,0:T(8,128)(2,1)} %bitcast.6, f32[1,256]{1,0:T(1,128)} %bitcast.7, bf16[2,256,2304]{2,1,0:T(8,128)(2,1)} %conv_hbm.1, bf16[256,1024]{1,0:T(8,128)(2,1)} %cond_hbm.1, bf16[84,256]{1,0:T(8,128)(2,1)} %out_hbm.1), custom_call_target="tpu_custom_call" | custom-call | tf_op jit(solution)/shard_map/pallas_call | solution.py:343
  21.2 0.7 %copy.9 = f32[1,84,4,128]{3,2,1,0:T(4,128)} copy(f32[1,84,4,128]{3,2,1,0:T(4,128)S(1)} %bitcast.4) | data formatting | bytes 344064

commit v5 on v4

v5 whole, which is shorter than its diff:
```python
import functools

import jax
import jax.numpy as jnp
from jax import lax
from jax.experimental import pallas as pl
from jax.experimental.pallas import tpu as pltpu
from jax.sharding import PartitionSpec as P

LEVELS = 64
MESH = pl.DeviceIdType.MESH

sigma_top = 1.0
sigma_low = 0.02
rho_power = 7.0


def level_sigma(level):
    top, low = sigma_top ** (1.0 / rho_power), sigma_low ** (1.0 / rho_power)
    root = top + level.astype(jnp.float32) / (LEVELS - 1) * (low - top)
    square = root * root
    return square * square * square * root


def kernel(
    sizes,
    levels_hbm,
    x_hbm,
    in_hbm,
    bias_hbm,
    conv_hbm,
    cond_hbm,
    out_hbm,
    result,
    levels,
    xs,
    in_t,
    in_pad,
    in_w,
    bias_row,
    conv_w,
    cond_w,
    out_w,
    cond,
    bias,
    g_one,
    g_two,
    state,
    drift,
    scaled,
    halo,
    recv,
    send,
    load_sem,
    halo_s,
    halo_r,
    chain_s,
    chain_r,
    ready,
):
    times, bands, C, R, W, HID = sizes
    pairs = R // 2
    W2 = 2 * W
    padded = scaled.shape[2]
    slot = lax.axis_index("tm")
    band = lax.axis_index("lat")
    has_low, has_high = band > 0, band < bands - 1
    has_next = slot < times - 1

    barrier = pltpu.get_barrier_semaphore()

    def greet(axis, index):
        pl.semaphore_signal(barrier, inc=1, device_id={axis: index}, device_id_type=MESH)

    pl.when(has_low)(lambda: greet("lat", band - 1))
    pl.when(has_high)(lambda: greet("lat", band + 1))
    pl.when(has_next)(lambda: greet("tm", slot + 1))

    loads = [
        pltpu.make_async_copy(source, target, load_sem.at[i])
        for i, (source, target) in enumerate(
            [
                (x_hbm, xs.at[pl.ds(0, C * R)]),
                (in_hbm, in_t),
                (bias_hbm, bias_row),
                (cond_hbm, cond_w),
                (conv_hbm.at[0], conv_w.at[0]),
                (conv_hbm.at[1], conv_w.at[1]),
                (out_hbm, out_w),
                (levels_hbm, levels),
            ]
        )
    ]
    for load in loads[-1:] + loads[:-1]:
        load.start()

    if padded > C:
        xs[C * R :, :] = jnp.zeros((padded * R - C * R, W), jnp.float32)
    drift[...] = jnp.zeros_like(drift)

    loads[7].wait()
    sigma = level_sigma(jnp.full((1, W2), levels[slot], jnp.int32))
    sigma_next = level_sigma(jnp.full((1, W2), levels[slot + 1], jnp.int32))
    variance = sigma * sigma + 0.25
    inverse = 1.0 / jnp.sqrt(variance)
    gain = (sigma_next - sigma) / sigma
    keep = gain * (sigma * sigma / variance)
    push = -0.5 * gain * sigma * inverse

    def own(q):
        return jnp.concatenate(
            [xs[pl.ds(2 * q + i, padded, stride=R), :] for i in range(2)], axis=1
        )

    loads[0].wait()
    for q in range(pairs):
        value = own(q)
        state[q] = value
        scaled[0, q] = (value * inverse).astype(jnp.bfloat16)

    def remote(source, target, send_sem, recv_sem, axis, index):
        return pltpu.make_async_remote_copy(
            src_ref=source,
            dst_ref=target,
            send_sem=send_sem,
            recv_sem=recv_sem,
            device_id={axis: index},
            device_id_type=MESH,
        )

    def down(source, s):
        return remote(source, halo.at[s, 1], halo_s.at[s, 1], halo_r.at[s, 1], "lat", band - 1)

    def up(source, s):
        return remote(source, halo.at[s, 0], halo_s.at[s, 0], halo_r.at[s, 0], "lat", band + 1)

    def onward(s, q):
        return remote(
            send.at[s, q], recv.at[s, q], chain_s.at[s, q], chain_r.at[s, q], "tm", slot + 1
        )

    pl.semaphore_wait(
        barrier,
        has_low.astype(jnp.int32) + has_high.astype(jnp.int32) + (slot > 0).astype(jnp.int32),
    )
    pl.when(has_low)(lambda: down(scaled.at[0, 0], 0).start())
    pl.when(has_high)(lambda: up(scaled.at[0, pairs - 1], 0).start())

    @pl.when(slot > 0)
    def _():
        pl.semaphore_signal(ready, inc=1, device_id={"tm": slot - 1}, device_id_type=MESH)

    in_pad[...] = jnp.zeros_like(in_pad)
    loads[1].wait()
    loads[2].wait()
    in_pad[0:C, :] = in_t[...].astype(jnp.float32)
    for j in range(HID // W):
        rows = pl.ds(j * W, W)
        in_w[rows, :] = in_pad[:, j * W : (j + 1) * W].T.astype(jnp.bfloat16)
        bias[rows, :] = jnp.broadcast_to(bias_row[:, j * W : (j + 1) * W], (W, W)).T

    half = cond_w.shape[0] // 2
    place = lax.broadcasted_iota(jnp.int32, (1, half), 1).astype(jnp.float32) / half
    frequency = jnp.exp(place * jnp.log(jnp.full((1, half), 100.0, jnp.float32)))
    phases = jnp.log(sigma[:, :1]) / 4.0 * frequency
    embedding = jnp.concatenate([jnp.cos(phases), jnp.sin(phases)], axis=1)
    embedding = jnp.broadcast_to(embedding, (W, 2 * half)).astype(jnp.bfloat16)
    loads[3].wait()
    conditions = jnp.dot(embedding, cond_w[...], preferred_element_type=jnp.float32)
    for j in range(4 * HID // W):
        block = conditions[:, j * W : (j + 1) * W].T
        is_scale = (j * W // HID) % 2 == 0
        cond[pl.ds(j * W, W), :] = block + 1.0 if is_scale else block

    def lanes(row, count):
        return pl.ds(pl.multiple_of(row * W, W), count * W)

    def shifts(target, chunk, halves):
        for i, half in enumerate(halves):
            value = half.astype(jnp.bfloat16)
            place = lanes(2 * chunk + i, 1)
            target[pl.ds(0, HID), place] = pltpu.roll(value, 1, 1)
            target[pl.ds(HID, HID), place] = value
            target[pl.ds(2 * HID, HID), place] = pltpu.roll(value, W - 1, 1)

    def project(chunks, values, insides=None):
        hidden = jnp.dot(
            in_w[:, :padded],
            jnp.concatenate(values, axis=1),
            preferred_element_type=jnp.float32,
        )
        for j, chunk in enumerate(chunks):
            halves = []
            for i in range(2):
                part = hidden[:, (2 * j + i) * W : (2 * j + i + 1) * W] + bias[...]
                halves.append(part if insides is None else jnp.where(insides[j], part, 0.0))
            shifts(g_one, chunk, halves)

    def convolve(source, layer, pair):
        rows = [source[:, lanes(2 * pair + a, 2)] for a in range(3)]
        return jnp.dot(
            conv_w[layer], jnp.concatenate(rows, axis=0), preferred_element_type=jnp.float32
        )

    def activated(response, layer, i):
        scale = cond[pl.ds(2 * layer * HID, HID), :]
        shift = cond[pl.ds((2 * layer + 1) * HID, HID), :]
        value = response[:, i * W : (i + 1) * W] * scale + shift
        part = 0.5 * value
        return part + part * jnp.tanh(part)

    def write(pair, value):
        for i in range(2):
            result[pl.ds(2 * pair + i, C, stride=R), :] = value[0:C, i * W : (i + 1) * W]

    loads[4].wait()
    loads[5].wait()
    loads[6].wait()
    pl.when(has_next)(lambda: pl.semaphore_wait(ready, 1))

    def sweep(s, _):
        @pl.when(s > 0)
        def _():
            for q in range(pairs):
                value = recv[0, q].astype(jnp.float32)
                state[q] = value
                scaled[1, q] = (value * inverse).astype(jnp.bfloat16)

        project(range(1, pairs + 1), [scaled[s, q] for q in range(pairs)])

        def layer_one(t, _):
            @pl.when(t == pairs - 1)
            def _():
                pl.when(has_low)(lambda: up(scaled.at[0, pairs - 1], s).wait_recv())
                pl.when(has_high)(lambda: down(scaled.at[0, 0], s).wait_recv())
                factor = jnp.where(jnp.full((1, W2), s, jnp.int32) > 0, inverse, 1.0)
                values = [
                    (halo[s, i].astype(jnp.float32) * factor).astype(jnp.bfloat16) for i in range(2)
                ]
                project((0, pairs + 1), values, (has_low, has_high))

            pair = jnp.where(t < pairs - 1, t + 1, jnp.where(t == pairs, pairs, 0))
            response = convolve(g_one, 0, pair)
            insides = (jnp.logical_or(pair > 0, has_low), jnp.logical_or(pair < pairs, has_high))
            halves = [jnp.where(insides[i], activated(response, 0, i), 0.0) for i in range(2)]
            shifts(g_two, pair, halves)
            return 0

        lax.fori_loop(0, pairs + 1, layer_one, 0)

        def layer_two(q, _):
            response = convolve(g_two, 1, q)
            halves = []
            for i in range(2):
                carried = g_two[pl.ds(HID, HID), lanes(2 * q + 1 + i, 1)].astype(jnp.float32)
                halves.append((carried + activated(response, 1, i)).astype(jnp.bfloat16))
            network = jnp.dot(
                out_w[...], jnp.concatenate(halves, axis=1), preferred_element_type=jnp.float32
            )
            drift[q, 0:C, :] = push * network
            return 0

        lax.fori_loop(0, pairs, layer_two, 0)

        for q in range(pairs):

            @pl.when(slot > s)
            def _():
                onward(s, q).wait_recv()

                @pl.when(s == 0)
                def _():
                    if q == 0:
                        pl.when(has_low)(lambda: down(recv.at[0, 0], 1).start())
                    if q == pairs - 1:
                        pl.when(has_high)(lambda: up(recv.at[0, pairs - 1], 1).start())

            change = keep * state[q] + drift[q]
            base = jnp.where(slot == s, state[q], recv[s, q].astype(jnp.float32))
            total = base + change
            send[s, q] = total.astype(jnp.bfloat16)
            pl.when(has_next)(lambda: onward(s, q).start())

            @pl.when(jnp.logical_or(s > 0, slot == 0))
            def _():
                write(q, total)

        return 0

    lax.fori_loop(0, jnp.where(slot > 0, 2, 1), sweep, 0)

    for s in range(2):

        @pl.when(slot >= s)
        def _():
            first, last = (scaled.at[0, 0], scaled.at[0, pairs - 1]) if s == 0 else (
                recv.at[0, 0],
                recv.at[0, pairs - 1],
            )
            pl.when(has_low)(lambda: down(first, s).wait_send())
            pl.when(has_high)(lambda: up(last, s).wait_send())

            @pl.when(has_next)
            def _():
                for q in range(pairs):
                    onward(s, q).wait_send()


def on_device(times, bands, trajectory, step_levels, in_weight, in_bias, conv_weight, cond_weight, out_weight):
    _, C, R, W = trajectory.shape
    HID = in_weight.shape[0]
    pairs = R // 2
    padded = -(-C // 16) * 16
    wide = -(-C // 128) * 128
    bf16, f32 = jnp.bfloat16, jnp.float32
    block = (pairs, padded, 2 * W)
    halo = (2, padded, 2 * W)
    anywhere = pl.BlockSpec(memory_space=pltpu.HBM)
    dma = pltpu.SemaphoreType.DMA
    result = pl.pallas_call(
        functools.partial(kernel, (times, bands, C, R, W, HID)),
        out_shape=jax.ShapeDtypeStruct((C * R, W), f32),
        in_specs=[anywhere] * 7,
        out_specs=pl.BlockSpec(memory_space=pltpu.VMEM),
        scratch_shapes=[
            pltpu.SMEM(step_levels.shape, jnp.int32),
            pltpu.VMEM((padded * R, W), f32),
            pltpu.VMEM((C, HID), bf16),
            pltpu.VMEM((wide, HID), f32),
            pltpu.VMEM((HID, wide), bf16),
            pltpu.VMEM((1, HID), f32),
            pltpu.VMEM(conv_weight.shape, bf16),
            pltpu.VMEM(cond_weight.shape, bf16),
            pltpu.VMEM(out_weight.shape, bf16),
            pltpu.VMEM((4 * HID, W), f32),
            pltpu.VMEM((HID, W), f32),
            pltpu.VMEM((3 * HID, (R + 4) * W), bf16),
            pltpu.VMEM((3 * HID, (R + 2) * W), bf16),
            pltpu.VMEM(block, f32),
            pltpu.VMEM(block, f32),
            pltpu.VMEM((2,) + block, bf16),
            pltpu.VMEM((2,) + halo, bf16),
            pltpu.VMEM((2,) + block, bf16),
            pltpu.VMEM((2,) + block, bf16),
            dma((8,)),
            dma((2, 2)),
            dma((2, 2)),
            dma((2, pairs)),
            dma((2, pairs)),
            pltpu.SemaphoreType.REGULAR,
        ],
        compiler_params=pltpu.CompilerParams(
            collective_id=0, has_side_effects=True, vmem_limit_bytes=32 * 1024 * 1024
        ),
    )(
        *(
            pltpu.with_memory_space_constraint(operand, pltpu.HBM)
            for operand in (
                step_levels,
                trajectory.reshape(C * R, W),
                in_weight.T,
                in_bias.reshape(1, HID),
                conv_weight,
                cond_weight,
                out_weight,
            )
        ),
    )
    return result.reshape(1, C, R, W)


def solution(mesh):
    in_specs = (P("tm", None, "lat", None), P(), P(), P(), P(), P(), P())
    out_specs = P("tm", None, "lat", None)
    return jax.shard_map(
        functools.partial(on_device, mesh.shape["tm"], mesh.shape["lat"]),
        mesh=mesh,
        in_specs=in_specs,
        out_specs=out_specs,
        check_vma=False,
    )
```

time: 22 us -> 23 us (1.045)
  Pallas kernels: 21.2 us -> 22.2 us
    pallas_call x1, Pallas kernels: 21.2 us -> 22.2 us  [on_device(): pl.pallas_call(functools.partial(kernel, (times, bands, C, R, W, HID)), o...]
where the time goes in v5:
time: 23 us; the launch traced here: 22.9 us
  Pallas kernels  22.2 us (97%)
  local copies, waits for them, and re-layouts  0.67 us (3%)
    pallas_call x1, Pallas kernels, on_device(): pl.pallas_call(functools.partial(kernel, (times, bands, C, R, W, HID)), o...  22.2 us
    unnamed x1, local copies, waits for them, and re-layouts  0.67 us

profile of v5, /device:TPU:27, one launch (start us, length us, event | category | flops | bytes accessed | tf_op | source)
XLA Modules:
  0.0 22.9 jit_solution(4227938878204633936)
XLA Ops:
  0.0 22.2 %shard_map.73 = f32[336,128]{1,0:T(8,128)S(1)} custom-call(s32[5]{0:T(128)} %levels_hbm.1, f32[336,128]{1,0:T(8,128)} %bitcast.5, bf16[84,256]{1,0:T(8,128)(2,1)} %bitcast.6, f32[1,256]{1,0:T(1,128)} %bitcast.7, bf16[2,256,2304]{2,1,0:T(8,128)(2,1)} %conv_hbm.1, bf16[256,1024]{1,0:T(8,128)(2,1)} %cond_hbm.1, bf16[84,256]{1,0:T(8,128)(2,1)} %out_hbm.1), custom_call_target="tpu_custom_call" | custom-call | tf_op jit(solution)/shard_map/pallas_call | solution.py:320
  22.2 0.7 %copy.9 = f32[1,84,4,128]{3,2,1,0:T(4,128)} copy(f32[1,84,4,128]{3,2,1,0:T(4,128)S(1)} %bitcast.4) | data formatting | bytes 344064

commit v6 on v4

--- a/solution.py
+++ b/solution.py
@@ -62,6 +62,7 @@
     halo_two_r,
     chain_two_s,
     chain_two_r,
+    ready,
 ):
     times, bands, C, R, W, HID = sizes
     pairs = R // 2
@@ -71,6 +72,15 @@
     band = lax.axis_index("lat")
     has_low, has_high = band > 0, band < bands - 1
     has_next = slot < times - 1
+
+    barrier = pltpu.get_barrier_semaphore()
+
+    def greet(axis, index):
+        pl.semaphore_signal(barrier, inc=1, device_id={axis: index}, device_id_type=MESH)
+
+    pl.when(has_low)(lambda: greet("lat", band - 1))
+    pl.when(has_high)(lambda: greet("lat", band + 1))
+    pl.when(has_next)(lambda: greet("tm", slot + 1))
 
     loads = [
         pltpu.make_async_copy(source, target, load_sem.at[i])
@@ -90,15 +100,6 @@
     for load in loads[-1:] + loads[:-1]:
         load.start()
 
-    barrier = pltpu.get_barrier_semaphore()
-
-    def greet(axis, index):
-        pl.semaphore_signal(barrier, inc=1, device_id={axis: index}, device_id_type=MESH)
-
-    pl.when(has_low)(lambda: greet("lat", band - 1))
-    pl.when(has_high)(lambda: greet("lat", band + 1))
-    pl.when(slot > 0)(lambda: greet("tm", slot - 1))
-
     if padded > C:
         xs[C * R :, :] = jnp.zeros((padded * R - C * R, W), jnp.float32)
     drift[...] = jnp.zeros_like(drift)
@@ -149,10 +150,15 @@
 
     pl.semaphore_wait(
         barrier,
-        has_low.astype(jnp.int32) + has_high.astype(jnp.int32) + has_next.astype(jnp.int32),
+        has_low.astype(jnp.int32) + has_high.astype(jnp.int32) + (slot > 0).astype(jnp.int32),
     )
     pl.when(has_low)(lambda: down(scaled.at[0], *first).start())
     pl.when(has_high)(lambda: up(scaled.at[pairs - 1], *first).start())
+
+    @pl.when(slot > 0)
+    def _():
+        pl.semaphore_signal(ready, inc=1, device_id={"tm": slot - 1}, device_id_type=MESH)
+
 
     in_pad[...] = jnp.zeros_like(in_pad)
     loads[1].wait()
@@ -236,20 +242,20 @@
         for pair, response in zip((0, pairs), convolve(g_one, 0, (0, pairs))):
             after_one(pair, response)
 
-    def changes(current):
+    def layer_two(q, current):
+        (response,) = convolve(g_two, 1, (q,))
         halves = []
-        for q, response in enumerate(convolve(g_two, 1, range(pairs))):
-            for i in range(2):
-                lanes = pl.ds((2 * q + 1 + i) * W, W)
-                carried = g_two[pl.ds(HID, HID), lanes].astype(jnp.float32)
-                halves.append((carried + activated(response, 1, i)).astype(jnp.bfloat16))
+        for i in range(2):
+            lanes = pl.ds((2 * q + 1 + i) * W, W)
+            carried = g_two[pl.ds(HID, HID), lanes].astype(jnp.float32)
+            halves.append((carried + activated(response, 1, i)).astype(jnp.bfloat16))
         network = jnp.dot(
             out_w[...], jnp.concatenate(halves, axis=1), preferred_element_type=jnp.float32
         )
-        for q in range(pairs):
-            drift[q, 0:C, :] = push * network[:, q * W2 : (q + 1) * W2]
-        for q in range(pairs):
-            yield q, keep * current(q) + drift[q]
+        drift[q, 0:C, :] = push * network
+        change = keep * current + drift[q]
+        drift[q] = change
+        return current + change
 
     def write(pair, value):
         for i in range(2):
@@ -262,13 +268,17 @@
     pl.when(has_low)(lambda: up(scaled.at[pairs - 1], *first).wait_recv())
     pl.when(has_high)(lambda: down(scaled.at[0], *first).wait_recv())
     outer(halo_one[0], halo_one[1])
-    for q, change in changes(own):
+    pl.when(has_next)(lambda: pl.semaphore_wait(ready, 1))
+    for q in range(pairs):
+        total = layer_two(q, own(q))
 
         @pl.when(slot == 0)
         def _():
-            total = own(q) + change
+            send_one[q] = total.astype(jnp.bfloat16)
+            pl.when(has_next)(lambda: onward(q, *chain_one).start())
             write(q, total)
-            send_one[q] = total.astype(jnp.bfloat16)
+
+    for q in range(pairs):
 
         @pl.when(slot > 0)
         def _():
@@ -277,9 +287,8 @@
                 pl.when(has_low)(lambda: down(recv_one.at[0], *second).start())
             if q == pairs - 1:
                 pl.when(has_high)(lambda: up(recv_one.at[pairs - 1], *second).start())
-            send_one[q] = (recv_one[q].astype(jnp.float32) + change).astype(jnp.bfloat16)
-
-        pl.when(has_next)(lambda: onward(q, *chain_one).start())
+            send_one[q] = (recv_one[q].astype(jnp.float32) + drift[q]).astype(jnp.bfloat16)
+            pl.when(has_next)(lambda: onward(q, *chain_one).start())
 
     @pl.when(slot > 0)
     def _():
@@ -293,22 +302,24 @@
         pl.when(has_high)(lambda: down(recv_one.at[0], *second).wait_recv())
         pl.when(has_low)(lambda: up(recv_one.at[pairs - 1], *second).wait_recv())
         outer(rescaled(halo_two[0]), rescaled(halo_two[1]))
-        for q, change in changes(state):
+        for q in range(pairs):
+            total = layer_two(q, state(q))
 
             @pl.when(slot == 1)
             def _():
-                total = state(q) + change
+                send_two[q] = total.astype(jnp.bfloat16)
+                pl.when(has_next)(lambda: onward(q, *chain_two).start())
                 write(q, total)
-                send_two[q] = total.astype(jnp.bfloat16)
+
+        for q in range(pairs):
 
             @pl.when(slot > 1)
             def _():
                 onward(q, *chain_two).wait_recv()
-                total = recv_two[q].astype(jnp.float32) + change
+                total = recv_two[q].astype(jnp.float32) + drift[q]
+                send_two[q] = total.astype(jnp.bfloat16)
+                pl.when(has_next)(lambda: onward(q, *chain_two).start())
                 write(q, total)
-                send_two[q] = total.astype(jnp.bfloat16)
-
-            pl.when(has_next)(lambda: onward(q, *chain_two).start())
 
     pl.when(has_low)(lambda: down(scaled.at[0], *first).wait_send())
     pl.when(has_high)(lambda: up(scaled.at[pairs - 1], *first).wait_send())
@@ -376,6 +387,7 @@
             dma((2,)),
             dma((pairs,)),
             dma((pairs,)),
+            pltpu.SemaphoreType.REGULAR,
         ],
         compiler_params=pltpu.CompilerParams(
             collective_id=0, has_side_effects=True, vmem_limit_bytes=32 * 1024 * 1024

time: 22 us -> 22.6 us (1.027)
  Pallas kernels: 21.2 us -> 21.8 us
    pallas_call x1, Pallas kernels: 21.2 us -> 21.8 us  [on_device(): pl.pallas_call(functools.partial(kernel, (times, bands, C, R, W, HID)), o...]
where the time goes in v6:
time: 22.6 us; the launch traced here: 22.5 us
  Pallas kernels  21.8 us (96%)
  local copies, waits for them, and re-layouts  0.67 us (3%)
    pallas_call x1, Pallas kernels, on_device(): pl.pallas_call(functools.partial(kernel, (times, bands, C, R, W, HID)), o...  21.8 us
    unnamed x1, local copies, waits for them, and re-layouts  0.67 us

profile of v6, /device:TPU:27, one launch (start us, length us, event | category | flops | bytes accessed | tf_op | source)
XLA Modules:
  0.0 22.5 jit_solution(9328852293564215475)
XLA Ops:
  0.0 21.8 %shard_map.73 = f32[336,128]{1,0:T(8,128)S(1)} custom-call(s32[5]{0:T(128)} %levels_hbm.1, f32[336,128]{1,0:T(8,128)} %bitcast.5, bf16[84,256]{1,0:T(8,128)(2,1)} %bitcast.6, f32[1,256]{1,0:T(1,128)} %bitcast.7, bf16[2,256,2304]{2,1,0:T(8,128)(2,1)} %conv_hbm.1, bf16[256,1024]{1,0:T(8,128)(2,1)} %cond_hbm.1, bf16[84,256]{1,0:T(8,128)(2,1)} %out_hbm.1), custom_call_target="tpu_custom_call" | custom-call | tf_op jit(solution)/shard_map/pallas_call | solution.py:354
  21.8 0.7 %copy.9 = f32[1,84,4,128]{3,2,1,0:T(4,128)} copy(f32[1,84,4,128]{3,2,1,0:T(4,128)S(1)} %bitcast.4) | data formatting | bytes 344064

commit v7 on v4

--- a/solution.py
+++ b/solution.py
@@ -72,6 +72,15 @@
     has_low, has_high = band > 0, band < bands - 1
     has_next = slot < times - 1
 
+    barrier = pltpu.get_barrier_semaphore()
+
+    def greet(axis, index):
+        pl.semaphore_signal(barrier, inc=1, device_id={axis: index}, device_id_type=MESH)
+
+    pl.when(has_low)(lambda: greet("lat", band - 1))
+    pl.when(has_high)(lambda: greet("lat", band + 1))
+    pl.when(slot > 0)(lambda: greet("tm", slot - 1))
+
     loads = [
         pltpu.make_async_copy(source, target, load_sem.at[i])
         for i, (source, target) in enumerate(
@@ -90,18 +99,8 @@
     for load in loads[-1:] + loads[:-1]:
         load.start()
 
-    barrier = pltpu.get_barrier_semaphore()
-
-    def greet(axis, index):
-        pl.semaphore_signal(barrier, inc=1, device_id={axis: index}, device_id_type=MESH)
-
-    pl.when(has_low)(lambda: greet("lat", band - 1))
-    pl.when(has_high)(lambda: greet("lat", band + 1))
-    pl.when(slot > 0)(lambda: greet("tm", slot - 1))
-
     if padded > C:
         xs[C * R :, :] = jnp.zeros((padded * R - C * R, W), jnp.float32)
-    drift[...] = jnp.zeros_like(drift)
 
     loads[7].wait()
     sigma = level_sigma(jnp.full((1, W2), levels[slot], jnp.int32))
@@ -154,6 +153,7 @@
     pl.when(has_low)(lambda: down(scaled.at[0], *first).start())
     pl.when(has_high)(lambda: up(scaled.at[pairs - 1], *first).start())
 
+    drift[...] = jnp.zeros_like(drift)
     in_pad[...] = jnp.zeros_like(in_pad)
     loads[1].wait()
     loads[2].wait()

time: 22 us -> 22 us (level)
  no operation moved by 1% of the time
where the time goes in v7:
time: 22 us; the launch traced here: 21.9 us
  Pallas kernels  21.2 us (96%)
  local copies, waits for them, and re-layouts  0.67 us (3%)
    pallas_call x1, Pallas kernels, on_device(): pl.pallas_call(functools.partial(kernel, (times, bands, C, R, W, HID)), o...  21.2 us
    unnamed x1, local copies, waits for them, and re-layouts  0.67 us

profile of v7, /device:TPU:27, one launch (start us, length us, event | category | flops | bytes accessed | tf_op | source)
XLA Modules:
  0.0 21.9 jit_solution(17270900938368954948)
XLA Ops:
  0.0 21.2 %shard_map.73 = f32[336,128]{1,0:T(8,128)S(1)} custom-call(s32[5]{0:T(128)} %levels_hbm.1, f32[336,128]{1,0:T(8,128)} %bitcast.5, bf16[84,256]{1,0:T(8,128)(2,1)} %bitcast.6, f32[1,256]{1,0:T(1,128)} %bitcast.7, bf16[2,256,2304]{2,1,0:T(8,128)(2,1)} %conv_hbm.1, bf16[256,1024]{1,0:T(8,128)(2,1)} %cond_hbm.1, bf16[84,256]{1,0:T(8,128)(2,1)} %out_hbm.1), custom_call_target="tpu_custom_call" | custom-call | tf_op jit(solution)/shard_map/pallas_call | solution.py:343
  21.2 0.7 %copy.9 = f32[1,84,4,128]{3,2,1,0:T(4,128)} copy(f32[1,84,4,128]{3,2,1,0:T(4,128)S(1)} %bitcast.4) | data formatting | bytes 344064
